TPU v7x, 32 devices: a whole 2x2x4 slice. The times are simulated.
32 devices in a mesh: tile: 16 (over z, y, core), layer: 2 (over x).
Axes of the slice: x: 2, y: 2, z: 4, core: 2. Of those that a mesh axis runs over, the one named last changes fastest.
Arguments:
- ensemble: float32 [64, 8, 8192], P(None, 'layer', 'tile'), may hold values from -6 to 6
- diff_x: float32 [8, 8192], P('layer', 'tile'), may hold values from 0.04 to 0.2
- diff_z: float32 [8, 8192], P('layer', 'tile'), may hold values from 0.04 to 0.2
- cour_x: float32 [8, 8192], P('layer', 'tile'), may hold values from -0.4 to 0.4
- cour_z: float32 [8, 8192], P('layer', 'tile'), may hold values from -0.4 to 0.4
- obs_cell: int32 [4, 512], replicated, may hold values from 0 to 65535
- obs_radius: int32 [4, 512], replicated, may hold values from 2048 to 8192
- obs_value: float32 [4, 512], replicated, may hold values from -6 to 6
- obs_var: float32 [4, 512], replicated, may hold values from 0.1 to 1
Outputs:
- posterior: float32 [64, 8, 8192], P(None, 'layer', 'tile')
Inputs may be any that keep to these rules, and one draw needn't show every extreme that they name: `obs_cell`: cells are drawn independently over the whole grid; two observations may share a cell.
All inputs are finite; a program needn't handle non-finite values.
Results may differ from a plain program's by a relative error of at most 0.00019.
Values sent between devices are 32-bit elements; how exact they have to be, the bound alone decides.
A program may use at most 64 MiB of HBM per device.

v0:
```python
import jax
import jax.numpy as jnp
from jax import lax
from jax.sharding import PartitionSpec as P


def extended(cells, sides, width):
    for axis, dim in sides:
        count = lax.axis_size(axis)
        ends = count - 1
        head = lax.slice_in_dim(cells, 0, width, axis=dim)
        tail = lax.slice_in_dim(cells, cells.shape[dim] - width, cells.shape[dim], axis=dim)
        cells = jnp.concatenate(
            [
                lax.ppermute(tail, axis, [(i, (i + 1) % count) for i in range(ends)]),
                cells,
                lax.ppermute(head, axis, [((i + 1) % count, i) for i in range(ends)]),
            ],
            axis=dim,
        )
    return cells


def increments(prior, value, variance):
    members = prior.shape[1]
    ymean = jnp.mean(prior, axis=1)
    anomaly = prior - ymean[:, None]
    spread = jnp.sum(anomaly * anomaly, axis=1) / (members - 1) + 1e-06
    shrink = variance / (spread + variance)
    postmean = spread * shrink * (ymean / spread + value / variance)
    delta = (postmean - ymean)[:, None] + (jnp.sqrt(shrink) - 1.0)[:, None] * anomaly
    factor = 1.0 / ((members - 1) * spread)
    return (anomaly, delta, factor)


def taper(positions, centres, radius):
    dist = jnp.abs(positions[None, :] - centres[:, None]).astype(jnp.float32)
    frac = jnp.maximum(1.0 - dist / radius[:, None].astype(jnp.float32), 0.0)
    return frac * frac


def pick_local(flat, cells, first_layer, first_col, depth, width, total_cols):
    rows = cells // total_cols - first_layer
    cols = cells % total_cols - first_col
    inside = (rows >= 0) & (rows < depth) & (cols >= 0) & (cols < width)
    index = jnp.where(inside, rows * width + cols, 0)
    values = jnp.take(flat, index, axis=1).T
    return jnp.where(inside[:, None], values, 0.0)


def gather_prior(picked):
    return lax.psum(picked, ("tile", "layer"))


def regress(state, anomaly, delta, weight):
    members, depth, width = state.shape
    count = anomaly.shape[0]
    xmean = jnp.mean(state, axis=0)
    deviation = (state - xmean[None]).reshape(members, depth * width)
    block = min(128, count)
    change = jnp.zeros((members, depth * width), jnp.float32)
    for start in range(0, count, block):
        cov = jnp.dot(anomaly[start : start + block], deviation, precision=lax.Precision.HIGHEST)
        gain = (
            cov.reshape(block, depth, width) * weight[start : start + block][:, None, :]
        ).reshape(block, depth * width)
        change = change + jnp.dot(
            delta[start : start + block].T, gain, precision=lax.Precision.HIGHEST
        )
    return state + change.reshape(members, depth, width)


def shards(ensemble, diff_x, diff_z, cour_x, cour_z, obs_cell, obs_radius, obs_value, obs_var):
    members, depth, width = ensemble.shape
    total_cols = width * lax.axis_size("tile")
    first_col = lax.axis_index("tile") * width
    first_layer = lax.axis_index("layer") * depth
    padded = extended(ensemble, (("tile", 2), ("layer", 1)), 1)
    centre = padded[:, 1:-1, 1:-1]
    upper = padded[:, :-2, 1:-1]
    lower = padded[:, 2:, 1:-1]
    west = padded[:, 1:-1, :-2]
    east = padded[:, 1:-1, 2:]
    state = (
        centre
        + diff_z * (upper - 2.0 * centre + lower)
        + diff_x * (west - 2.0 * centre + east)
        - 0.5 * cour_z * (lower - upper)
        - 0.5 * cour_x * (east - west)
    )
    positions = first_col + jnp.arange(width, dtype=jnp.int32)
    batches, count = obs_cell.shape
    for batch in range(batches):
        cells = obs_cell[batch]
        flat = state.reshape(members, depth * width)
        prior = gather_prior(
            pick_local(flat, cells, first_layer, first_col, depth, width, total_cols)
        )
        anomaly, delta, factor = increments(prior, obs_value[batch], obs_var[batch])
        weight = taper(positions, cells % total_cols, obs_radius[batch]) * factor[:, None]
        state = regress(state, anomaly, delta, weight)
    return state


def solution(mesh):
    in_specs = (
        P(None, "layer", "tile"),
        P("layer", "tile"),
        P("layer", "tile"),
        P("layer", "tile"),
        P("layer", "tile"),
        P(),
        P(),
        P(),
        P(),
    )
    out_specs = P(None, "layer", "tile")
    return jax.shard_map(shards, mesh=mesh, in_specs=in_specs, out_specs=out_specs, check_vma=False)
```

profile of v0, /device:TPU:0, one launch (start us, length us, event | category | flops | bytes accessed | tf_op | source)
XLA Modules:
  0.0 608.1 jit_solution(5944438097676178219)
XLA Ops:
  6.5 1.2 copy.114
  7.9 1.3 collective-permute-start.1
  9.2 3.0 collective-permute-start
  18.0 1.3 collective-permute-start.3
  19.3 4.9 collective-permute-start.2
  24.8 1.1 collective-permute-done.3
  26.0 1.8 collective-permute-done.2
  28.6 1.0 gather_fusion
  30.5 125.8 %all-reduce.5.cloned.1.call-done = f32[512,64]{0,1:T(8,128)} async-done(((f32[512,64]{0,1:T(8,128)}), f32[512,64]{0,1:T(8,128)}) %all-reduce.5.cloned.1.call-update) | async-done | bytes 131088 | tf_op jit(solution)/shard_map/psum | solution.py:52
  159.9 1.0 convolution_multiply_fusion.14
  160.9 1.3 copy.123
  163.3 1.3 copy.125
  165.6 1.3 copy.127
  167.0 1.2 fusion.54
  168.3 1.2 convolution_add_fusion.11
  169.5 1.3 convolution_add_fusion.10
  170.8 1.2 convolution_add_fusion.9
  172.8 1.0 gather_fusion.1
  175.6 121.4 %all-reduce.7.cloned.1.call-done = f32[512,64]{0,1:T(8,128)} async-done(((f32[512,64]{0,1:T(8,128)}), f32[512,64]{0,1:T(8,128)}) %all-reduce.7.cloned.1.call-update) | async-done | bytes 131088 | tf_op jit(solution)/shard_map/psum | solution.py:52
  302.0 2.0 convolution_multiply_fusion.10
  304.0 1.3 copy.135
  306.3 1.3 copy.137
  308.7 1.3 copy.139
  310.0 1.2 fusion.49
  311.3 1.3 convolution_add_fusion.8
  312.5 1.2 convolution_add_fusion.7
  313.8 1.2 convolution_add_fusion.6
  315.8 1.0 gather_fusion.2
  318.6 121.3 %all-reduce.9.cloned.1.call-done = f32[512,64]{0,1:T(8,128)} async-done(((f32[512,64]{0,1:T(8,128)}), f32[512,64]{0,1:T(8,128)}) %all-reduce.9.cloned.1.call-update) | async-done | bytes 131088 | tf_op jit(solution)/shard_map/psum | solution.py:52
  444.9 1.0 convolution_multiply_fusion.6
  445.9 1.3 copy.147
  448.3 1.3 copy.149
  450.6 1.3 copy.151
  452.0 1.2 fusion.44
  453.2 1.2 convolution_add_fusion.5
  454.5 1.3 convolution_add_fusion.4
  455.8 1.2 convolution_add_fusion.3
  457.5 1.3 gather_fusion.3
  460.3 121.6 %all-reduce.11.cloned.1.call-done = f32[512,64]{0,1:T(8,128)} async-done(((f32[512,64]{0,1:T(8,128)}), f32[512,64]{0,1:T(8,128)}) %all-reduce.11.cloned.1.call-update) | async-done | bytes 131088 | tf_op jit(solution)/shard_map/psum | solution.py:52
  586.9 2.0 convolution_multiply_fusion.2
  588.9 1.3 copy.159
  591.2 1.3 copy.161
  593.6 1.3 copy.163
  594.9 1.2 fusion.39
  596.2 1.3 convolution_add_fusion.2
  597.4 1.2 convolution_add_fusion.1
  598.7 1.2 convolution_add_fusion
  600.0 1.1 copy.165
  (188 shorter events, 41.6 us)
Async XLA Ops:
  6.5 149.8 %all-reduce.5.cloned.1.call-start = ((), (), s32[]{:S(2)}) async-start(), calls=%async_computation | async-start | bytes 262144 | tf_op jit(solution)/shard_map/psum | solution.py:52
  7.8 4.4 copy-start.30
  7.9 10.0 %collective-permute-start.1 = (f32[64,4,1]{2,0,1:T(8,128)S(1)}, f32[64,4,1]{2,0,1:T(8,128)S(1)}, u32[]{:S(2)}, u32[]{:S(2)}) collective-permute-start(f32[64,4,1]{2,0,1:T(8,128)S(1)} %get-tuple-element.53), channel_id=1, source_target_pairs={{2,0},{4,2},{6,4},{8,6},{10,8},{12,10},{14,12},{16,14},{18,16},{20... | collective-permute-start | bytes 3080 | tf_op jit(solution)/shard_map/ppermute | solution.py:17
  9.2 8.7 %collective-permute-start = (f32[64,4,1]{2,0,1:T(8,128)S(1)}, f32[64,4,1]{2,0,1:T(8,128)S(1)}, u32[]{:S(2)}, u32[]{:S(2)}) collective-permute-start(f32[64,4,1]{2,0,1:T(8,128)S(1)} %get-tuple-element.52), channel_id=1, source_target_pairs={{0,2},{2,4},{4,6},{6,8},{8,10},{10,12},{12,14},{14,16},{16,18},{18... | collective-permute-start | bytes 3080 | tf_op jit(solution)/shard_map/ppermute | solution.py:15
  13.9 1.2 copy-start.31
  15.2 0.7 copy-start.32
  15.8 0.7 copy-start.33
  16.5 0.7 copy-start.34
  16.5 0.7 copy-start.35
  18.0 7.9 %collective-permute-start.3 = (f32[64,1,514]{2,0,1:T(8,128)S(1)}, f32[64,1,514]{2,0,1:T(8,128)S(1)}, u32[]{:S(2)}, u32[]{:S(2)}) collective-permute-start(f32[64,1,514]{2,0,1:T(8,128)S(1)} %get-tuple-element.51), channel_id=1, source_target_pairs={{1,0},{3,2},{5,4},{7,6},{9,8},{11,10},{13,12},{15,14},{17,16},{19,... | collective-permute-start | bytes 394760 | tf_op jit(solution)/shard_map/ppermute | solution.py:17
  19.3 8.4 %collective-permute-start.2 = (f32[64,1,514]{2,0,1:T(8,128)S(1)}, f32[64,1,514]{2,0,1:T(8,128)S(1)}, u32[]{:S(2)}, u32[]{:S(2)}) collective-permute-start(f32[64,1,514]{2,0,1:T(8,128)S(1)} %get-tuple-element.50), channel_id=1, source_target_pairs={{0,1},{2,3},{4,5},{6,7},{8,9},{10,11},{12,13},{14,15},{16,17},{18,... | collective-permute-start | bytes 394760 | tf_op jit(solution)/shard_map/ppermute | solution.py:15
  24.2 3.5 copy-start.18
  24.2 3.5 copy-start.19
  30.5 266.5 %all-reduce.7.cloned.1.call-start = ((), (), s32[]{:S(2)}) async-start(), calls=%async_computation.1 | async-start | bytes 262144 | tf_op jit(solution)/shard_map/psum | solution.py:52
  156.4 1.0 copy-start.12
  165.6 1.4 copy-start.20
  165.6 1.4 copy-start.21
  167.0 1.3 copy-start
  168.3 1.3 copy-start.4
  169.5 1.3 copy-start.8
  172.2 0.7 copy-start.17
  175.3 264.6 %all-reduce.9.cloned.1.call-start = ((), (), s32[]{:S(2)}) async-start(), calls=%async_computation.2 | async-start | bytes 262144 | tf_op jit(solution)/shard_map/psum | solution.py:52
  297.0 1.0 copy-start.13
  298.0 0.7 copy-start.40
  298.7 0.7 copy-start.29
  298.7 0.7 copy-start.26
  310.0 1.3 copy-start.1
  311.3 1.3 copy-start.5
  312.5 1.3 copy-start.9
  315.2 0.7 copy-start.16
  317.0 0.7 copy-start.45
  318.4 263.5 %all-reduce.11.cloned.1.call-start = ((), (), s32[]{:S(2)}) async-start(), calls=%async_computation.3 | async-start | bytes 262144 | tf_op jit(solution)/shard_map/psum | solution.py:52
  440.0 1.0 copy-start.14
  441.0 0.7 copy-start.39
  441.0 0.7 copy-start.38
  442.3 0.7 copy-start.28
  442.3 0.7 copy-start.25
  450.6 1.4 copy-start.22
  450.6 1.4 copy-start.23
  452.0 1.3 copy-start.2
  453.2 1.3 copy-start.6
  454.5 1.3 copy-start.10
  581.8 1.0 copy-start.15
  582.9 0.7 copy-start.37
  582.9 0.7 copy-start.36
  594.9 1.3 copy-start.3
  596.2 1.3 copy-start.7
  597.4 1.3 copy-start.11
  (8 other events, 5.1 us)
Sparse Core Ops, SparseCore 0:
  30.6 125.7 all-reduce.4
  175.4 121.4 all-reduce.6
  318.5 121.4 all-reduce.8
  460.4 121.4 all-reduce.10
where the time goes:
time: 617 us; the launch traced here: 608 us
  waiting for transfers between devices  493 us (80%)
  matrix products  38.2 us (6%)
  local copies, waits for them, and re-layouts  35.8 us (6%)
  other arithmetic  15.7 us (3%)
  between operations  14.4 us (2%)
  starting transfers between devices  11 us (2%)
    psum x4, waiting for transfers between devices, gather_prior(): return lax.psum(picked, ('tile', 'layer'))  490 us
    dot_general x16, matrix products, regress(): jnp.dot(delta[start:start + block].T, gain, precision=lax.Precision.HIGHEST)  20 us
    dot_general x16, matrix products, regress(): jnp.dot(anomaly[start:start + block], deviation, precision=lax.Precision....  18.2 us
    mul x16, local copies, waits for them, and re-layouts, regress(): cov.reshape(block, depth, width) * weight[start:start + block][:, None, :]  17.2 us
  transfers between devices with their start and end apart: 8, of which 6 were waited for; matrix products, arithmetic and copies ran while one was open for 1% of the time, Pallas kernels for 0%

commit v1 on v0

v1 whole, which is shorter than its diff:
```python
import functools

import jax
import jax.numpy as jnp
from jax import lax
from jax.experimental import pallas as pl
from jax.experimental.pallas import tpu as pltpu
from jax.sharding import PartitionSpec as P

MESH = pl.DeviceIdType.MESH
LANES = 128


def split_cell(cells, total):
    if total & (total - 1) == 0:
        return cells >> (total.bit_length() - 1), cells & (total - 1)
    return cells // total, cells % total


def halves(value):
    high = value.astype(jnp.bfloat16)
    return high, (value - high.astype(jnp.float32)).astype(jnp.bfloat16)


def gather_kernel(
    tiles, layers, ens, diff_x, diff_z, cour_x, cour_z, obs_cell, state, prior,
    cells, edge_w, edge_e, halo_w, halo_e, halo_u, halo_d, part, in_core, in_plane, in_line,
    halo_send, halo_recv, core_sem, plane_send, plane_recv, line_send, line_recv,
):
    members, depth, width = ens.shape
    batches, count = obs_cell.shape
    tile, layer = lax.axis_index("tile"), lax.axis_index("layer")
    core, row, line = tile % 2, (tile // 2) % 2, tile // 4
    plane_n, line_n = layers * 2, tiles // 4
    spot = layer * 2 + row
    pair = (tile + 1 - 2 * core, layer)

    def plane_at(index):
        return (line * 4 + (index % 2) * 2 + core, index // 2)

    def line_at(index):
        return (index * 4 + row * 2 + core, layer)

    greeted = [pair, ((tile + 1) % tiles, layer), ((tile + tiles - 1) % tiles, layer)]
    greeted += [(tile, (layer + 1) % layers), (tile, (layer + layers - 1) % layers)]
    greeted += [plane_at((spot + j) % plane_n) for j in range(1, plane_n)]
    greeted += [line_at((line + j) % line_n) for j in range(1, line_n)]
    barrier = pltpu.get_barrier_semaphore()
    for device in greeted:
        pl.semaphore_signal(barrier, inc=1, device_id=device, device_id_type=MESH)

    lane = lax.broadcasted_iota(jnp.int32, (members, LANES), 1)
    west = jnp.zeros((members, LANES), jnp.float32)
    east = jnp.zeros((members, LANES), jnp.float32)
    for l in range(depth):
        x = ens[:, l, :]
        cells[l] = x
        west = jnp.where(lane == l, x[:, 0:1], west)
        east = jnp.where(lane == l, x[:, width - 1 : width], east)
    edge_w[...] = west
    edge_e[...] = east
    pl.semaphore_wait(barrier, len(greeted))

    def remote(src, dst, send, recv, device):
        return pltpu.make_async_remote_copy(
            src_ref=src, dst_ref=dst, send_sem=send, recv_sem=recv, device_id=device, device_id_type=MESH
        )

    up, down = layer > 0, layer < layers - 1
    before, after = tile > 0, tile < tiles - 1
    moves = (
        (down, up, remote(cells.at[depth - 1], halo_u, halo_send.at[0], halo_recv.at[0], (tile, lax.rem(layer + 1, layers))), halo_u),
        (up, down, remote(cells.at[0], halo_d, halo_send.at[1], halo_recv.at[1], (tile, lax.rem(layer + layers - 1, layers))), halo_d),
        (after, before, remote(edge_e, halo_w, halo_send.at[2], halo_recv.at[2], (lax.rem(tile + 1, tiles), layer)), halo_w),
        (before, after, remote(edge_w, halo_e, halo_send.at[3], halo_recv.at[3], (lax.rem(tile + tiles - 1, tiles), layer)), halo_e),
    )
    for sends, receives, copy, place in moves:
        pl.when(sends)(copy.start)

        @pl.when(jnp.logical_not(receives))
        def _(place=place):
            place[...] = jnp.zeros_like(place)

    for sends, receives, copy, place in moves:
        pl.when(receives)(copy.wait_recv)

    column = lax.broadcasted_iota(jnp.int32, (members, width), 1)
    parts = []
    for l in range(depth):
        x = cells[l]
        upper = halo_u[...] if l == 0 else cells[l - 1]
        lower = halo_d[...] if l == depth - 1 else cells[l + 1]
        left = jnp.where(column == 0, halo_w[:, l : l + 1], pltpu.roll(x, 1, 1))
        right = jnp.where(column == width - 1, halo_e[:, l : l + 1], pltpu.roll(x, width - 1, 1))
        dx, dz = diff_x[l : l + 1, :], diff_z[l : l + 1, :]
        cx, cz = 0.5 * cour_x[l : l + 1, :], 0.5 * cour_z[l : l + 1, :]
        new = (
            x * (1.0 - 2.0 * dz - 2.0 * dx)
            + upper * (dz + cz)
            + lower * (dz - cz)
            + left * (dx + cx)
            + right * (dx - cx)
        )
        state[l] = new
        parts.extend(halves(new))
    stacked = jnp.concatenate(parts, axis=0)

    blocks = count // LANES
    place = lax.broadcasted_iota(jnp.int32, (width, count), 0)
    for b in range(batches):
        rows, cols = split_cell(obs_cell[b : b + 1, :], tiles * width)
        rows, cols = rows - layer * depth, cols - tile * width
        hot = jnp.where(place == cols, 1.0, 0.0).astype(jnp.bfloat16)
        picked = jnp.dot(stacked, hot, preferred_element_type=jnp.float32)
        total = jnp.zeros((members, count), jnp.float32)
        for l in range(depth):
            both = picked[2 * l * members : (2 * l + 1) * members] + picked[(2 * l + 1) * members : (2 * l + 2) * members]
            total = jnp.where(rows == l, both, total)
        for k in range(blocks):
            part[pl.ds((b * blocks + k) * members, members), :] = total[:, k * LANES : (k + 1) * LANES]

    half = part.shape[0] // 2
    mine = pl.multiple_of(core * half, 8)
    other = pl.multiple_of((1 - core) * half, 8)
    copy = remote(part.at[pl.ds(other, half)], in_core, core_sem.at[0], core_sem.at[1], pair)
    copy.start()
    copy.wait_recv()
    core_out = copy
    part[pl.ds(mine, half), :] += in_core[...]

    size = half // plane_n
    base = pl.multiple_of(mine + spot * size, 8)
    plane_out = []
    for j in range(1, plane_n):
        to = (spot + j) % plane_n
        copy = remote(
            part.at[pl.ds(pl.multiple_of(mine + to * size, 8), size)], in_plane.at[j - 1],
            plane_send.at[j - 1], plane_recv.at[j - 1], plane_at(to),
        )
        copy.start()
        plane_out.append(copy)
    total = part[pl.ds(base, size), :]
    for j in range(1, plane_n):
        plane_out[j - 1].wait_recv()
        total = total + in_plane[j - 1]
    part[pl.ds(base, size), :] = total

    scatter = size % (8 * line_n) == 0
    piece = size // line_n if scatter else size
    own = pl.multiple_of(base + line * piece, 8) if scatter else base
    line_out = []
    for j in range(1, line_n):
        to = (line + j) % line_n
        start = pl.multiple_of(base + to * piece, 8) if scatter else base
        copy = remote(part.at[pl.ds(start, piece)], in_line.at[j - 1], line_send.at[j - 1], line_recv.at[j - 1], line_at(to))
        copy.start()
        line_out.append(copy)
    total = part[pl.ds(own, piece), :]
    for j in range(1, line_n):
        line_out[j - 1].wait_recv()
        total = total + in_line[j - 1]
    prior[pl.ds(own, piece), :] = total

    back = []
    if scatter:
        for j in range(1, line_n):
            view = prior.at[pl.ds(own, piece)]
            k = line_n - 1 + j - 1
            copy = remote(view, view, line_send.at[k], line_recv.at[k], line_at((line + j) % line_n))
            copy.start()
            back.append(copy)
        for copy in back:
            copy.wait_recv()
    spread = []
    for j in range(1, plane_n):
        view = prior.at[pl.ds(base, size)]
        k = plane_n - 1 + j - 1
        copy = remote(view, view, plane_send.at[k], plane_recv.at[k], plane_at((spot + j) % plane_n))
        copy.start()
        spread.append(copy)
    for copy in spread:
        copy.wait_recv()
    view = prior.at[pl.ds(mine, half)]
    last = remote(view, view, core_sem.at[2], core_sem.at[3], pair)
    last.start()
    last.wait_recv()
    for copy in [core_out, last] + plane_out + line_out + back + spread:
        copy.wait_send()
    for sends, receives, copy, place in moves:
        pl.when(sends)(copy.wait_send)


def update_kernel(total_cols, width, state, prior, obs_cell, obs_radius, obs_value, obs_var, out, layers_ref, later_ref):
    depth, members, _ = state.shape
    batches, count = obs_cell.shape
    blocks = count // LANES
    first = lax.axis_index("tile") * width
    layers_ref[...] = state[...]
    for b in range(batches):
        for k in range(blocks):
            later_ref[b, :, k * LANES : (k + 1) * LANES] = prior[pl.ds((b * blocks + k) * members, members), :]
    centre = split_cell(obs_cell[...], total_cols)[1].astype(jnp.float32)
    inverse = 1.0 / obs_radius[...].astype(jnp.float32)
    upright = jnp.concatenate([centre, inverse], axis=0).T
    grid = (first + lax.broadcasted_iota(jnp.int32, (1, width), 1)).astype(jnp.float32)

    for b in range(batches):
        y = later_ref[b]
        value, variance = obs_value[b : b + 1, :], obs_var[b : b + 1, :]
        ymean = jnp.sum(y, axis=0, keepdims=True) * (1.0 / members)
        anomaly = y - ymean
        spread = jnp.sum(anomaly * anomaly, axis=0, keepdims=True) / (members - 1) + 1e-06
        shrink = variance / (spread + variance)
        postmean = spread * shrink * (ymean / spread + value / variance)
        delta = (postmean - ymean) + (jnp.sqrt(shrink) - 1.0) * anomaly
        delta = delta * (1.0 / ((members - 1) * spread))
        d_high, d_low = halves(delta)
        d_both = jnp.concatenate([d_high, d_low], axis=0)
        y_high = anomaly.astype(jnp.bfloat16).astype(jnp.float32)
        y_low = anomaly - y_high
        lhs = jnp.concatenate([y_high, y_high, y_low, y_low], axis=0).T.astype(jnp.bfloat16)
        here, scale = upright[:, b : b + 1], upright[:, batches + b : batches + b + 1]

        def taper(positions):
            frac = jnp.maximum(1.0 - jnp.abs(positions - here) * scale, 0.0)
            return frac * frac

        def change(x, weight):
            x_high, x_low = halves(x - jnp.sum(x, axis=0, keepdims=True) * (1.0 / members))
            rhs = jnp.concatenate([x_high, x_low, x_high, x_low], axis=0)
            gain = jnp.dot(lhs, rhs, preferred_element_type=jnp.float32) * weight
            g_high, g_low = halves(gain)
            one = jnp.dot(d_both, g_high, preferred_element_type=jnp.float32)
            two = jnp.dot(d_high, g_low, preferred_element_type=jnp.float32)
            return one[:members] + one[members:] + two

        for c in range(b + 1, batches):
            later_ref[c] += change(later_ref[c], taper(centre[c : c + 1, :]))
        weight = taper(grid)
        for l in range(depth):
            x = layers_ref[l]
            x = x + change(x, weight)
            if b == batches - 1:
                out[:, l, :] = x
            else:
                layers_ref[l] = x


def shards(ensemble, diff_x, diff_z, cour_x, cour_z, obs_cell, obs_radius, obs_value, obs_var):
    members, depth, width = ensemble.shape
    batches, count = obs_cell.shape
    tiles, layers = lax.axis_size("tile"), lax.axis_size("layer")
    rows = batches * count * members // LANES
    plane_n, line_n = layers * 2, tiles // 4
    size = rows // 2 // plane_n
    piece = size // line_n if size % (8 * line_n) == 0 else size
    vmem = pl.BlockSpec(memory_space=pltpu.VMEM)
    f32 = jnp.float32
    state, prior = pl.pallas_call(
        functools.partial(gather_kernel, tiles, layers),
        out_shape=(jax.ShapeDtypeStruct((depth, members, width), f32), jax.ShapeDtypeStruct((rows, LANES), f32)),
        in_specs=[vmem] * 6,
        out_specs=(vmem, vmem),
        scratch_shapes=[
            pltpu.VMEM((depth, members, width), f32),
            pltpu.VMEM((members, LANES), f32),
            pltpu.VMEM((members, LANES), f32),
            pltpu.VMEM((members, LANES), f32),
            pltpu.VMEM((members, LANES), f32),
            pltpu.VMEM((members, width), f32),
            pltpu.VMEM((members, width), f32),
            pltpu.VMEM((rows, LANES), f32),
            pltpu.VMEM((rows // 2, LANES), f32),
            pltpu.VMEM((plane_n - 1, size, LANES), f32),
            pltpu.VMEM((line_n - 1, piece, LANES), f32),
            pltpu.SemaphoreType.DMA((4,)),
            pltpu.SemaphoreType.DMA((4,)),
            pltpu.SemaphoreType.DMA((4,)),
            pltpu.SemaphoreType.DMA((2 * plane_n - 2,)),
            pltpu.SemaphoreType.DMA((2 * plane_n - 2,)),
            pltpu.SemaphoreType.DMA((2 * line_n - 2,)),
            pltpu.SemaphoreType.DMA((2 * line_n - 2,)),
        ],
        compiler_params=pltpu.CompilerParams(collective_id=0, has_side_effects=True, vmem_limit_bytes=40 * 2**20),
        name="gather_prior",
    )(ensemble, diff_x, diff_z, cour_x, cour_z, obs_cell)
    return pl.pallas_call(
        functools.partial(update_kernel, tiles * width, width),
        out_shape=jax.ShapeDtypeStruct((members, depth, width), f32),
        in_specs=[vmem] * 6,
        out_specs=vmem,
        scratch_shapes=[
            pltpu.VMEM((depth, members, width), f32),
            pltpu.VMEM((batches, members, count), f32),
        ],
        compiler_params=pltpu.CompilerParams(vmem_limit_bytes=40 * 2**20),
        name="update",
    )(state, prior, obs_cell, obs_radius, obs_value, obs_var)


def solution(mesh):
    in_specs = (
        P(None, "layer", "tile"),
        P("layer", "tile"),
        P("layer", "tile"),
        P("layer", "tile"),
        P("layer", "tile"),
        P(),
        P(),
        P(),
        P(),
    )
    out_specs = P(None, "layer", "tile")
    return jax.shard_map(shards, mesh=mesh, in_specs=in_specs, out_specs=out_specs, check_vma=False)
```

time: 617 us -> 47.2 us (0.08); the launches traced: 608 us -> 46.7 us
  waiting for transfers between devices: 493 us -> 0 us
  Pallas kernels: 0 us -> 42.2 us
  matrix products: 38.2 us -> 0 us
  local copies, waits for them, and re-layouts: 35.8 us -> 4.53 us
  other arithmetic: 15.7 us -> 0 us
  between operations: 14.4 us -> 0.04 us
  starting transfers between devices: 11 us -> 0 us
    psum x4 -> x0, waiting for transfers between devices: 490 us -> none  [gather_prior(): return lax.psum(picked, ('tile', 'layer'))]
    pallas_call x0 -> x2, Pallas kernels: none -> 42.2 us  [the longest x1 30.5 us: shards(): pl.pallas_call(functools.partial(gather_kernel, tiles, layers), out_shape...]
    dot_general x32 -> x0, matrix products: 38.2 us -> none  [the longest x16 20 us: regress(): jnp.dot(delta[start:start + block].T, gain, precision=lax.Precision.HIGHEST)]
    mul x16 -> x0, local copies, waits for them, and re-layouts: 17.2 us -> none  [regress(): cov.reshape(block, depth, width) * weight[start:start + block][:, None, :]]
    ppermute x4 -> x0, starting transfers between devices: 10.5 us -> none  [the longest x2 7.9 us: extended(): lax.ppermute(tail, axis, [(i, (i + 1) % count) for i in range(ends)])]
  transfers between devices with their start and end apart: 8 -> 0, of which waited for: 6 -> 0; matrix products, arithmetic and copies ran while one was open for 1% -> 0% of each run, Pallas kernels for 0% -> 0%
where the time goes in v1:
time: 47.2 us; the launch traced here: 46.7 us
  Pallas kernels  42.2 us (89%)
  local copies, waits for them, and re-layouts  4.53 us (10%)
    pallas_call x1, Pallas kernels, shards(): pl.pallas_call(functools.partial(gather_kernel, tiles, layers), out_shape...  30.5 us
    pallas_call x1, Pallas kernels, shards(): pl.pallas_call(functools.partial(update_kernel, tiles * width, width), ou...  11.7 us
    unnamed x18, local copies, waits for them, and re-layouts  4.53 us

profile of v1, /device:TPU:0, one launch (start us, length us, event | category | flops | bytes accessed | tf_op | source)
XLA Modules:
  0.0 46.7 jit_solution(11526135114775216501)
XLA Ops:
  0.0 0.0 copy-start
  0.0 1.0 %copy-done = f32[64,4,512]{2,1,0:T(4,128)S(1)} copy-done((f32[64,4,512]{2,1,0:T(4,128)S(1)}, f32[64,4,512]{2,1,0:T(4,128)}, u32[]{:S(2)}) %copy-start) | copy-done | bytes 524312
  1.0 0.0 copy-start.1
  1.0 0.7 %copy-done.1 = s32[4,512]{1,0:T(4,128)S(1)} copy-done((s32[4,512]{1,0:T(4,128)S(1)}, s32[4,512]{1,0:T(4,128)}, u32[]{:S(2)}) %copy-start.1) | copy-done | bytes 8216
  1.7 0.0 copy-start.2
  1.7 0.7 %copy-done.2 = f32[4,512]{1,0:T(4,128)S(1)} copy-done((f32[4,512]{1,0:T(4,128)S(1)}, f32[4,512]{1,0:T(4,128)}, u32[]{:S(2)}) %copy-start.2) | copy-done | bytes 8216
  2.4 0.0 copy-start.3
  2.4 0.7 %copy-done.3 = f32[4,512]{1,0:T(4,128)S(1)} copy-done((f32[4,512]{1,0:T(4,128)S(1)}, f32[4,512]{1,0:T(4,128)}, u32[]{:S(2)}) %copy-start.3) | copy-done | bytes 8216
  3.1 0.0 copy-start.4
  3.1 0.7 %copy-done.4 = f32[4,512]{1,0:T(4,128)S(1)} copy-done((f32[4,512]{1,0:T(4,128)S(1)}, f32[4,512]{1,0:T(4,128)}, u32[]{:S(2)}) %copy-start.4) | copy-done | bytes 8216
  3.8 0.0 copy-start.5
  3.8 0.7 %copy-done.5 = f32[4,512]{1,0:T(4,128)S(1)} copy-done((f32[4,512]{1,0:T(4,128)S(1)}, f32[4,512]{1,0:T(4,128)}, u32[]{:S(2)}) %copy-start.5) | copy-done | bytes 8216
  4.5 0.0 copy-start.6
  4.5 0.0 copy-start.7
  4.5 0.0 copy-start.8
  4.5 30.5 %gather_prior.1 = (f32[4,64,512]{2,1,0:T(8,128)S(1)}, f32[1024,128]{1,0:T(8,128)S(1)}) custom-call(f32[64,4,512]{2,1,0:T(4,128)S(1)} %copy-done, f32[4,512]{1,0:T(4,128)S(1)} %copy-done.2, f32[4,512]{1,0:T(4,128)S(1)} %copy-done.3, f32[4,512]{1,0:T(4,128)S(1)} %copy-done.4, f32[4,512]{1,0:T(4,128)S(1)} %copy-done.5, s32[4,512]{1,0:T(4,128)S(1)} %copy-done.1), custom_call_target="tpu_custom_call" | custom-call | tf_op jit(solution)/shard_map/gather_prior/pallas_call | solution.py:259
  35.0 0.0 copy-done.6
  35.0 0.0 copy-done.7
  35.0 0.0 copy-done.8
  35.0 11.7 %update.1 = f32[64,4,512]{2,1,0:T(4,128)} custom-call(f32[4,64,512]{2,1,0:T(8,128)S(1)} %get-tuple-element.7.state, f32[1024,128]{1,0:T(8,128)S(1)} %get-tuple-element.8.prior, s32[4,512]{1,0:T(4,128)S(1)} %copy-done.1, s32[4,512]{1,0:T(4,128)S(1)} %copy-done.6, f32[4,512]{1,0:T(4,128)S(1)} %copy-done.7, f32[4,512]{1,0:T(4,128)S(1)} %copy-done.8), custom_call_target="tpu_custom_call" | custom-call | tf_op jit(solution)/shard_map/update/pallas_call | solution.py:287
Async XLA Ops:
  0.0 1.0 %copy-start = (f32[64,4,512]{2,1,0:T(4,128)S(1)}, f32[64,4,512]{2,1,0:T(4,128)}, u32[]{:S(2)}) copy-start(f32[64,4,512]{2,1,0:T(4,128)} %ens.1) | copy-start | bytes 1572868
  1.0 0.7 %copy-start.1 = (s32[4,512]{1,0:T(4,128)S(1)}, s32[4,512]{1,0:T(4,128)}, u32[]{:S(2)}) copy-start(s32[4,512]{1,0:T(4,128)} %obs_cell.3) | copy-start | bytes 24580
  1.7 0.7 %copy-start.2 = (f32[4,512]{1,0:T(4,128)S(1)}, f32[4,512]{1,0:T(4,128)}, u32[]{:S(2)}) copy-start(f32[4,512]{1,0:T(4,128)} %diff_x.1) | copy-start | bytes 24580
  2.4 0.7 %copy-start.3 = (f32[4,512]{1,0:T(4,128)S(1)}, f32[4,512]{1,0:T(4,128)}, u32[]{:S(2)}) copy-start(f32[4,512]{1,0:T(4,128)} %diff_z.1) | copy-start | bytes 24580
  3.1 0.7 %copy-start.4 = (f32[4,512]{1,0:T(4,128)S(1)}, f32[4,512]{1,0:T(4,128)}, u32[]{:S(2)}) copy-start(f32[4,512]{1,0:T(4,128)} %cour_x.1) | copy-start | bytes 24580
  3.8 0.7 %copy-start.5 = (f32[4,512]{1,0:T(4,128)S(1)}, f32[4,512]{1,0:T(4,128)}, u32[]{:S(2)}) copy-start(f32[4,512]{1,0:T(4,128)} %cour_z.1) | copy-start | bytes 24580
  4.5 30.5 %copy-start.6 = (s32[4,512]{1,0:T(4,128)S(1)}, s32[4,512]{1,0:T(4,128)}, u32[]{:S(2)}) copy-start(s32[4,512]{1,0:T(4,128)} %obs_radius.1) | copy-start | bytes 24580
  4.5 30.5 %copy-start.7 = (f32[4,512]{1,0:T(4,128)S(1)}, f32[4,512]{1,0:T(4,128)}, u32[]{:S(2)}) copy-start(f32[4,512]{1,0:T(4,128)} %obs_value.1) | copy-start | bytes 24580
  4.5 30.5 %copy-start.8 = (f32[4,512]{1,0:T(4,128)S(1)}, f32[4,512]{1,0:T(4,128)}, u32[]{:S(2)}) copy-start(f32[4,512]{1,0:T(4,128)} %obs_var.1) | copy-start | bytes 24580

commit v2 on v1

--- a/solution.py
+++ b/solution.py
@@ -23,10 +23,18 @@
 
 
 def gather_kernel(
-    tiles, layers, ens, diff_x, diff_z, cour_x, cour_z, obs_cell, state, prior,
-    cells, edge_w, edge_e, halo_w, halo_e, halo_u, halo_d, part, in_core, in_plane, in_line,
-    halo_send, halo_recv, core_sem, plane_send, plane_recv, line_send, line_recv,
+    tiles, layers, ens_in, dx_in, dz_in, cx_in, cz_in, cell_in, state, prior,
+    ens, diff_x, diff_z, cour_x, cour_z, obs_cell, load_sem,
+    cells, edge_w, edge_e, halo_w, halo_e, halo_u, halo_d, coef_up, coef_down, coef_u, coef_d,
+    part, in_core, in_plane, in_line, halo_send, halo_recv, core_sem, plane_send, plane_recv, line_send, line_recv,
 ):
+    loads = []
+    for i, (src, dst) in enumerate(
+        ((ens_in, ens), (dz_in, diff_z), (cz_in, cour_z), (dx_in, diff_x), (cx_in, cour_x), (cell_in, obs_cell))
+    ):
+        copy = pltpu.make_async_copy(src, dst, load_sem.at[i])
+        copy.start()
+        loads.append(copy)
     members, depth, width = ens.shape
     batches, count = obs_cell.shape
     tile, layer = lax.axis_index("tile"), lax.axis_index("layer")
@@ -49,6 +57,8 @@
     for device in greeted:
         pl.semaphore_signal(barrier, inc=1, device_id=device, device_id_type=MESH)
 
+    for copy in loads:
+        copy.wait()
     lane = lax.broadcasted_iota(jnp.int32, (members, LANES), 1)
     west = jnp.zeros((members, LANES), jnp.float32)
     east = jnp.zeros((members, LANES), jnp.float32)
@@ -59,6 +69,9 @@
         east = jnp.where(lane == l, x[:, width - 1 : width], east)
     edge_w[...] = west
     edge_e[...] = east
+    tall = coef_up.shape
+    coef_up[...] = jnp.broadcast_to(diff_z[0:1, :] + 0.5 * cour_z[0:1, :], tall)
+    coef_down[...] = jnp.broadcast_to(diff_z[depth - 1 : depth, :] - 0.5 * cour_z[depth - 1 : depth, :], tall)
     pl.semaphore_wait(barrier, len(greeted))
 
     def remote(src, dst, send, recv, device):
@@ -68,125 +81,160 @@
 
     up, down = layer > 0, layer < layers - 1
     before, after = tile > 0, tile < tiles - 1
-    moves = (
-        (down, up, remote(cells.at[depth - 1], halo_u, halo_send.at[0], halo_recv.at[0], (tile, lax.rem(layer + 1, layers))), halo_u),
-        (up, down, remote(cells.at[0], halo_d, halo_send.at[1], halo_recv.at[1], (tile, lax.rem(layer + layers - 1, layers))), halo_d),
-        (after, before, remote(edge_e, halo_w, halo_send.at[2], halo_recv.at[2], (lax.rem(tile + 1, tiles), layer)), halo_w),
-        (before, after, remote(edge_w, halo_e, halo_send.at[3], halo_recv.at[3], (lax.rem(tile + tiles - 1, tiles), layer)), halo_e),
+    above, below = (tile, lax.rem(layer + layers - 1, layers)), (tile, lax.rem(layer + 1, layers))
+    ahead, behind = (lax.rem(tile + 1, tiles), layer), (lax.rem(tile + tiles - 1, tiles), layer)
+
+    def move(i, sends, receives, src, dst, device):
+        return sends, receives, remote(src, dst, halo_send.at[i], halo_recv.at[i], device), dst
+
+    small = (
+        move(0, after, before, edge_e, halo_w, ahead),
+        move(1, before, after, edge_w, halo_e, behind),
+        move(2, down, up, coef_down, coef_u, below),
+        move(3, up, down, coef_up, coef_d, above),
     )
-    for sends, receives, copy, place in moves:
+    large = (
+        move(4, down, up, cells.at[depth - 1], halo_u, below),
+        move(5, up, down, cells.at[0], halo_d, above),
+    )
+    for sends, receives, copy, place in small:
         pl.when(sends)(copy.start)
+    for sends, receives, copy, place in small + large:
 
         @pl.when(jnp.logical_not(receives))
         def _(place=place):
             place[...] = jnp.zeros_like(place)
 
-    for sends, receives, copy, place in moves:
+    for sends, receives, copy, place in small:
         pl.when(receives)(copy.wait_recv)
 
     column = lax.broadcasted_iota(jnp.int32, (members, width), 1)
+    levels = list(range(depth)) + [-1, depth]
     parts = []
     for l in range(depth):
         x = cells[l]
-        upper = halo_u[...] if l == 0 else cells[l - 1]
-        lower = halo_d[...] if l == depth - 1 else cells[l + 1]
         left = jnp.where(column == 0, halo_w[:, l : l + 1], pltpu.roll(x, 1, 1))
         right = jnp.where(column == width - 1, halo_e[:, l : l + 1], pltpu.roll(x, width - 1, 1))
         dx, dz = diff_x[l : l + 1, :], diff_z[l : l + 1, :]
         cx, cz = 0.5 * cour_x[l : l + 1, :], 0.5 * cour_z[l : l + 1, :]
-        new = (
-            x * (1.0 - 2.0 * dz - 2.0 * dx)
-            + upper * (dz + cz)
-            + lower * (dz - cz)
-            + left * (dx + cx)
-            + right * (dx - cx)
-        )
+        new = x * (1.0 - 2.0 * dz - 2.0 * dx) + left * (dx + cx) + right * (dx - cx)
+        if l > 0:
+            new = new + cells[l - 1] * (dz + cz)
+        if l < depth - 1:
+            new = new + cells[l + 1] * (dz - cz)
         state[l] = new
         parts.extend(halves(new))
+    parts.extend(halves(cells[0] * coef_u[0:1, :]))
+    parts.extend(halves(cells[depth - 1] * coef_d[0:1, :]))
     stacked = jnp.concatenate(parts, axis=0)
 
     blocks = count // LANES
+    extent = blocks * members
+    half = extent // 2
+    size = half // plane_n
+    scatter = size % (8 * line_n) == 0
+    piece = size // line_n if scatter else size
     place = lax.broadcasted_iota(jnp.int32, (width, count), 0)
-    for b in range(batches):
+
+    def start_of(b, *steps):
+        total = b * extent
+        for index, length in steps:
+            total = total + index * length
+        return pl.multiple_of(total, 8)
+
+    every = range(batches)
+    core_out, plane_out, line_out, line_back, plane_back, core_back = ([[] for _ in every] for _ in range(6))
+    for b in every:
         rows, cols = split_cell(obs_cell[b : b + 1, :], tiles * width)
         rows, cols = rows - layer * depth, cols - tile * width
         hot = jnp.where(place == cols, 1.0, 0.0).astype(jnp.bfloat16)
         picked = jnp.dot(stacked, hot, preferred_element_type=jnp.float32)
         total = jnp.zeros((members, count), jnp.float32)
-        for l in range(depth):
-            both = picked[2 * l * members : (2 * l + 1) * members] + picked[(2 * l + 1) * members : (2 * l + 2) * members]
+        for i, l in enumerate(levels):
+            both = picked[2 * i * members : (2 * i + 1) * members] + picked[(2 * i + 1) * members : (2 * i + 2) * members]
             total = jnp.where(rows == l, both, total)
         for k in range(blocks):
             part[pl.ds((b * blocks + k) * members, members), :] = total[:, k * LANES : (k + 1) * LANES]
-
-    half = part.shape[0] // 2
-    mine = pl.multiple_of(core * half, 8)
-    other = pl.multiple_of((1 - core) * half, 8)
-    copy = remote(part.at[pl.ds(other, half)], in_core, core_sem.at[0], core_sem.at[1], pair)
-    copy.start()
-    copy.wait_recv()
-    core_out = copy
-    part[pl.ds(mine, half), :] += in_core[...]
-
-    size = half // plane_n
-    base = pl.multiple_of(mine + spot * size, 8)
-    plane_out = []
-    for j in range(1, plane_n):
-        to = (spot + j) % plane_n
-        copy = remote(
-            part.at[pl.ds(pl.multiple_of(mine + to * size, 8), size)], in_plane.at[j - 1],
-            plane_send.at[j - 1], plane_recv.at[j - 1], plane_at(to),
-        )
+        copy = remote(part.at[pl.ds(start_of(b, (1 - core, half)), half)], in_core.at[b], core_sem.at[b, 0], core_sem.at[b, 1], pair)
         copy.start()
-        plane_out.append(copy)
-    total = part[pl.ds(base, size), :]
-    for j in range(1, plane_n):
-        plane_out[j - 1].wait_recv()
-        total = total + in_plane[j - 1]
-    part[pl.ds(base, size), :] = total
-
-    scatter = size % (8 * line_n) == 0
-    piece = size // line_n if scatter else size
-    own = pl.multiple_of(base + line * piece, 8) if scatter else base
-    line_out = []
-    for j in range(1, line_n):
-        to = (line + j) % line_n
-        start = pl.multiple_of(base + to * piece, 8) if scatter else base
-        copy = remote(part.at[pl.ds(start, piece)], in_line.at[j - 1], line_send.at[j - 1], line_recv.at[j - 1], line_at(to))
+        core_out[b].append(copy)
+
+    for b in every:
+        core_out[b][0].wait_recv()
+        part[pl.ds(start_of(b, (core, half)), half), :] += in_core[b]
+        for j in range(1, plane_n):
+            to = (spot + j) % plane_n
+            copy = remote(
+                part.at[pl.ds(start_of(b, (core, half), (to, size)), size)], in_plane.at[b, j - 1],
+                plane_send.at[b, j - 1], plane_recv.at[b, j - 1], plane_at(to),
+            )
+            copy.start()
+            plane_out[b].append(copy)
+    for b in every:
+        base = start_of(b, (core, half), (spot, size))
+        total = part[pl.ds(base, size), :]
+        for j in range(1, plane_n):
+            plane_out[b][j - 1].wait_recv()
+            total = total + in_plane[b, j - 1]
+        part[pl.ds(base, size), :] = total
+        for j in range(1, line_n):
+            to = (line + j) % line_n
+            start = start_of(b, (core, half), (spot, size), (to, piece)) if scatter else base
+            copy = remote(part.at[pl.ds(start, piece)], in_line.at[b, j - 1], line_send.at[b, j - 1], line_recv.at[b, j - 1], line_at(to))
+            copy.start()
+            line_out[b].append(copy)
+    for sends, receives, copy, _ in large:
+        pl.when(sends)(copy.start)
+
+    def spread_plane(b):
+        view = prior.at[pl.ds(start_of(b, (core, half), (spot, size)), size)]
+        for j in range(1, plane_n):
+            k = plane_n - 1 + j - 1
+            copy = remote(view, view, plane_send.at[b, k], plane_recv.at[b, k], plane_at((spot + j) % plane_n))
+            copy.start()
+            plane_back[b].append(copy)
+
+    for b in every:
+        own = start_of(b, (core, half), (spot, size), (line, piece)) if scatter else start_of(b, (core, half), (spot, size))
+        total = part[pl.ds(own, piece), :]
+        for j in range(1, line_n):
+            line_out[b][j - 1].wait_recv()
+            total = total + in_line[b, j - 1]
+        prior[pl.ds(own, piece), :] = total
+        if scatter:
+            view = prior.at[pl.ds(own, piece)]
+            for j in range(1, line_n):
+                k = line_n - 1 + j - 1
+                copy = remote(view, view, line_send.at[b, k], line_recv.at[b, k], line_at((line + j) % line_n))
+                copy.start()
+                line_back[b].append(copy)
+        else:
+            spread_plane(b)
+    if scatter:
+        for b in every:
+            for copy in line_back[b]:
+                copy.wait_recv()
+            spread_plane(b)
+
+    for sends, receives, copy, _ in large:
+        pl.when(receives)(copy.wait_recv)
+    state[0] += halo_u[...] * (diff_z[0:1, :] + 0.5 * cour_z[0:1, :])
+    state[depth - 1] += halo_d[...] * (diff_z[depth - 1 : depth, :] - 0.5 * cour_z[depth - 1 : depth, :])
+
+    for b in every:
+        for copy in plane_back[b]:
+            copy.wait_recv()
+        view = prior.at[pl.ds(start_of(b, (core, half)), half)]
+        copy = remote(view, view, core_sem.at[b, 2], core_sem.at[b, 3], pair)
         copy.start()
-        line_out.append(copy)
-    total = part[pl.ds(own, piece), :]
-    for j in range(1, line_n):
-        line_out[j - 1].wait_recv()
-        total = total + in_line[j - 1]
-    prior[pl.ds(own, piece), :] = total
-
-    back = []
-    if scatter:
-        for j in range(1, line_n):
-            view = prior.at[pl.ds(own, piece)]
-            k = line_n - 1 + j - 1
-            copy = remote(view, view, line_send.at[k], line_recv.at[k], line_at((line + j) % line_n))
-            copy.start()
-            back.append(copy)
-        for copy in back:
-            copy.wait_recv()
-    spread = []
-    for j in range(1, plane_n):
-        view = prior.at[pl.ds(base, size)]
-        k = plane_n - 1 + j - 1
-        copy = remote(view, view, plane_send.at[k], plane_recv.at[k], plane_at((spot + j) % plane_n))
-        copy.start()
-        spread.append(copy)
-    for copy in spread:
-        copy.wait_recv()
-    view = prior.at[pl.ds(mine, half)]
-    last = remote(view, view, core_sem.at[2], core_sem.at[3], pair)
-    last.start()
-    last.wait_recv()
-    for copy in [core_out, last] + plane_out + line_out + back + spread:
-        copy.wait_send()
-    for sends, receives, copy, place in moves:
+        core_back[b].append(copy)
+    for b in every:
+        core_back[b][0].wait_recv()
+    for group in (core_out, plane_out, line_out, line_back, plane_back, core_back):
+        for copies in group:
+            for copy in copies:
+                copy.wait_send()
+    for sends, receives, copy, _ in small + large:
         pl.when(sends)(copy.wait_send)
 
 
@@ -252,34 +300,37 @@
     tiles, layers = lax.axis_size("tile"), lax.axis_size("layer")
     rows = batches * count * members // LANES
     plane_n, line_n = layers * 2, tiles // 4
-    size = rows // 2 // plane_n
+    half = rows // batches // 2
+    size = half // plane_n
     piece = size // line_n if size % (8 * line_n) == 0 else size
     vmem = pl.BlockSpec(memory_space=pltpu.VMEM)
     f32 = jnp.float32
+    dma = pltpu.SemaphoreType.DMA
     state, prior = pl.pallas_call(
         functools.partial(gather_kernel, tiles, layers),
         out_shape=(jax.ShapeDtypeStruct((depth, members, width), f32), jax.ShapeDtypeStruct((rows, LANES), f32)),
-        in_specs=[vmem] * 6,
+        in_specs=[pl.BlockSpec(memory_space=pltpu.HBM)] * 6,
         out_specs=(vmem, vmem),
         scratch_shapes=[
+            pltpu.VMEM((members, depth, width), f32),
+            *[pltpu.VMEM((depth, width), f32)] * 4,
+            pltpu.VMEM((batches, count), jnp.int32),
+            dma((6,)),
             pltpu.VMEM((depth, members, width), f32),
-            pltpu.VMEM((members, LANES), f32),
-            pltpu.VMEM((members, LANES), f32),
-            pltpu.VMEM((members, LANES), f32),
-            pltpu.VMEM((members, LANES), f32),
-            pltpu.VMEM((members, width), f32),
-            pltpu.VMEM((members, width), f32),
+            *[pltpu.VMEM((members, LANES), f32)] * 4,
+            *[pltpu.VMEM((members, width), f32)] * 2,
+            *[pltpu.VMEM((8, width), f32)] * 4,
             pltpu.VMEM((rows, LANES), f32),
-            pltpu.VMEM((rows // 2, LANES), f32),
-            pltpu.VMEM((plane_n - 1, size, LANES), f32),
-            pltpu.VMEM((line_n - 1, piece, LANES), f32),
-            pltpu.SemaphoreType.DMA((4,)),
-            pltpu.SemaphoreType.DMA((4,)),
-            pltpu.SemaphoreType.DMA((4,)),
-            pltpu.SemaphoreType.DMA((2 * plane_n - 2,)),
-            pltpu.SemaphoreType.DMA((2 * plane_n - 2,)),
-            pltpu.SemaphoreType.DMA((2 * line_n - 2,)),
-            pltpu.SemaphoreType.DMA((2 * line_n - 2,)),
+            pltpu.VMEM((batches, half, LANES), f32),
+            pltpu.VMEM((batches, plane_n - 1, size, LANES), f32),
+            pltpu.VMEM((batches, line_n - 1, piece, LANES), f32),
+            dma((6,)),
+            dma((6,)),
+            dma((batches, 4)),
+            dma((batches, 2 * plane_n - 2)),
+            dma((batches, 2 * plane_n - 2)),
+            dma((batches, 2 * line_n - 2)),
+            dma((batches, 2 * line_n - 2)),
         ],
         compiler_params=pltpu.CompilerParams(collective_id=0, has_side_effects=True, vmem_limit_bytes=40 * 2**20),
         name="gather_prior",

time: 47.2 us -> 45.6 us (0.966)
  Pallas kernels: 42.2 us -> 40.6 us
    pallas_call x1, Pallas kernels: 30.5 us -> 28.9 us  [shards(): pl.pallas_call(functools.partial(gather_kernel, tiles, layers), out_shape...]
where the time goes in v2:
time: 45.6 us; the launch traced here: 45.1 us
  Pallas kernels  40.6 us (89%)
  local copies, waits for them, and re-layouts  4.53 us (10%)
    pallas_call x1, Pallas kernels, shards(): pl.pallas_call(functools.partial(gather_kernel, tiles, layers), out_shape...  28.9 us
    pallas_call x1, Pallas kernels, shards(): pl.pallas_call(functools.partial(update_kernel, tiles * width, width), ou...  11.7 us
    unnamed x18, local copies, waits for them, and re-layouts  4.53 us

profile of v2, /device:TPU:0, one launch (start us, length us, event | category | flops | bytes accessed | tf_op | source)
XLA Modules:
  0.0 45.1 jit_solution(14942239858271779471)
XLA Ops:
  0.0 0.0 copy-start
  0.0 1.0 %copy-done = f32[64,4,512]{2,1,0:T(4,128)S(1)} copy-done((f32[64,4,512]{2,1,0:T(4,128)S(1)}, f32[64,4,512]{2,1,0:T(4,128)}, u32[]{:S(2)}) %copy-start) | copy-done | bytes 524312
  1.0 0.0 copy-start.1
  1.0 0.7 %copy-done.1 = s32[4,512]{1,0:T(4,128)S(1)} copy-done((s32[4,512]{1,0:T(4,128)S(1)}, s32[4,512]{1,0:T(4,128)}, u32[]{:S(2)}) %copy-start.1) | copy-done | bytes 8216
  1.7 0.0 copy-start.2
  1.7 0.7 %copy-done.2 = f32[4,512]{1,0:T(4,128)S(1)} copy-done((f32[4,512]{1,0:T(4,128)S(1)}, f32[4,512]{1,0:T(4,128)}, u32[]{:S(2)}) %copy-start.2) | copy-done | bytes 8216
  2.4 0.0 copy-start.3
  2.4 0.7 %copy-done.3 = f32[4,512]{1,0:T(4,128)S(1)} copy-done((f32[4,512]{1,0:T(4,128)S(1)}, f32[4,512]{1,0:T(4,128)}, u32[]{:S(2)}) %copy-start.3) | copy-done | bytes 8216
  3.1 0.0 copy-start.4
  3.1 0.7 %copy-done.4 = f32[4,512]{1,0:T(4,128)S(1)} copy-done((f32[4,512]{1,0:T(4,128)S(1)}, f32[4,512]{1,0:T(4,128)}, u32[]{:S(2)}) %copy-start.4) | copy-done | bytes 8216
  3.8 0.0 copy-start.5
  3.8 0.7 %copy-done.5 = f32[4,512]{1,0:T(4,128)S(1)} copy-done((f32[4,512]{1,0:T(4,128)S(1)}, f32[4,512]{1,0:T(4,128)}, u32[]{:S(2)}) %copy-start.5) | copy-done | bytes 8216
  4.5 0.0 copy-start.6
  4.5 0.0 copy-start.7
  4.5 0.0 copy-start.8
  4.5 28.9 %gather_prior.1 = (f32[4,64,512]{2,1,0:T(8,128)S(1)}, f32[1024,128]{1,0:T(8,128)S(1)}) custom-call(f32[64,4,512]{2,1,0:T(4,128)S(1)} %copy-done, f32[4,512]{1,0:T(4,128)S(1)} %copy-done.2, f32[4,512]{1,0:T(4,128)S(1)} %copy-done.3, f32[4,512]{1,0:T(4,128)S(1)} %copy-done.4, f32[4,512]{1,0:T(4,128)S(1)} %copy-done.5, s32[4,512]{1,0:T(4,128)S(1)} %copy-done.1), custom_call_target="tpu_custom_call" | custom-call | tf_op jit(solution)/shard_map/gather_prior/pallas_call | solution.py:309
  33.4 0.0 copy-done.6
  33.4 0.0 copy-done.7
  33.4 0.0 copy-done.8
  33.4 11.7 %update.1 = f32[64,4,512]{2,1,0:T(4,128)} custom-call(f32[4,64,512]{2,1,0:T(8,128)S(1)} %get-tuple-element.7.state, f32[1024,128]{1,0:T(8,128)S(1)} %get-tuple-element.8.prior, s32[4,512]{1,0:T(4,128)S(1)} %copy-done.1, s32[4,512]{1,0:T(4,128)S(1)} %copy-done.6, f32[4,512]{1,0:T(4,128)S(1)} %copy-done.7, f32[4,512]{1,0:T(4,128)S(1)} %copy-done.8), custom_call_target="tpu_custom_call" | custom-call | tf_op jit(solution)/shard_map/update/pallas_call | solution.py:338
Async XLA Ops:
  0.0 1.0 %copy-start = (f32[64,4,512]{2,1,0:T(4,128)S(1)}, f32[64,4,512]{2,1,0:T(4,128)}, u32[]{:S(2)}) copy-start(f32[64,4,512]{2,1,0:T(4,128)} %ens_in.1) | copy-start | bytes 1572868
  1.0 0.7 %copy-start.1 = (s32[4,512]{1,0:T(4,128)S(1)}, s32[4,512]{1,0:T(4,128)}, u32[]{:S(2)}) copy-start(s32[4,512]{1,0:T(4,128)} %obs_cell.1) | copy-start | bytes 24580
  1.7 0.7 %copy-start.2 = (f32[4,512]{1,0:T(4,128)S(1)}, f32[4,512]{1,0:T(4,128)}, u32[]{:S(2)}) copy-start(f32[4,512]{1,0:T(4,128)} %dx_in.1) | copy-start | bytes 24580
  2.4 0.7 %copy-start.3 = (f32[4,512]{1,0:T(4,128)S(1)}, f32[4,512]{1,0:T(4,128)}, u32[]{:S(2)}) copy-start(f32[4,512]{1,0:T(4,128)} %dz_in.1) | copy-start | bytes 24580
  3.1 0.7 %copy-start.4 = (f32[4,512]{1,0:T(4,128)S(1)}, f32[4,512]{1,0:T(4,128)}, u32[]{:S(2)}) copy-start(f32[4,512]{1,0:T(4,128)} %cx_in.1) | copy-start | bytes 24580
  3.8 0.7 %copy-start.5 = (f32[4,512]{1,0:T(4,128)S(1)}, f32[4,512]{1,0:T(4,128)}, u32[]{:S(2)}) copy-start(f32[4,512]{1,0:T(4,128)} %cz_in.1) | copy-start | bytes 24580
  4.5 28.9 %copy-start.6 = (s32[4,512]{1,0:T(4,128)S(1)}, s32[4,512]{1,0:T(4,128)}, u32[]{:S(2)}) copy-start(s32[4,512]{1,0:T(4,128)} %obs_radius.1) | copy-start | bytes 24580
  4.5 28.9 %copy-start.7 = (f32[4,512]{1,0:T(4,128)S(1)}, f32[4,512]{1,0:T(4,128)}, u32[]{:S(2)}) copy-start(f32[4,512]{1,0:T(4,128)} %obs_value.1) | copy-start | bytes 24580
  4.5 28.9 %copy-start.8 = (f32[4,512]{1,0:T(4,128)S(1)}, f32[4,512]{1,0:T(4,128)}, u32[]{:S(2)}) copy-start(f32[4,512]{1,0:T(4,128)} %obs_var.1) | copy-start | bytes 24580

commit v3 on v2

--- a/solution.py
+++ b/solution.py
@@ -23,8 +23,8 @@
 
 
 def gather_kernel(
-    tiles, layers, ens_in, dx_in, dz_in, cx_in, cz_in, cell_in, state, prior,
-    ens, diff_x, diff_z, cour_x, cour_z, obs_cell, load_sem,
+    tiles, layers, ens_in, dx_in, dz_in, cx_in, cz_in, cell_in, state_out, prior,
+    state, state_sem, ens, diff_x, diff_z, cour_x, cour_z, obs_cell, load_sem,
     cells, edge_w, edge_e, halo_w, halo_e, halo_u, halo_d, coef_up, coef_down, coef_u, coef_d,
     part, in_core, in_plane, in_line, halo_send, halo_recv, core_sem, plane_send, plane_recv, line_send, line_recv,
 ):
@@ -220,6 +220,8 @@
         pl.when(receives)(copy.wait_recv)
     state[0] += halo_u[...] * (diff_z[0:1, :] + 0.5 * cour_z[0:1, :])
     state[depth - 1] += halo_d[...] * (diff_z[depth - 1 : depth, :] - 0.5 * cour_z[depth - 1 : depth, :])
+    keep = pltpu.make_async_copy(state, state_out, state_sem)
+    keep.start()
 
     for b in every:
         for copy in plane_back[b]:
@@ -236,14 +238,29 @@
                 copy.wait_send()
     for sends, receives, copy, _ in small + large:
         pl.when(sends)(copy.wait_send)
-
-
-def update_kernel(total_cols, width, state, prior, obs_cell, obs_radius, obs_value, obs_var, out, layers_ref, later_ref):
-    depth, members, _ = state.shape
+    keep.wait()
+
+
+def update_kernel(
+    total_cols, width, state_in, prior_in, cell_in, radius_in, value_in, var_in, out,
+    layers_ref, later_ref, prior, obs_cell, obs_radius, obs_value, obs_var, load_sem,
+):
+    loads = []
+    for i, (src, dst) in enumerate(
+        (
+            (cell_in, obs_cell), (radius_in, obs_radius), (value_in, obs_value), (var_in, obs_var),
+            (prior_in, prior), (state_in, layers_ref),
+        )
+    ):
+        copy = pltpu.make_async_copy(src, dst, load_sem.at[i])
+        copy.start()
+        loads.append(copy)
+    depth, members, _ = layers_ref.shape
     batches, count = obs_cell.shape
     blocks = count // LANES
     first = lax.axis_index("tile") * width
-    layers_ref[...] = state[...]
+    for copy in loads[:-1]:
+        copy.wait()
     for b in range(batches):
         for k in range(blocks):
             later_ref[b, :, k * LANES : (k + 1) * LANES] = prior[pl.ds((b * blocks + k) * members, members), :]
@@ -285,6 +302,8 @@
         for c in range(b + 1, batches):
             later_ref[c] += change(later_ref[c], taper(centre[c : c + 1, :]))
         weight = taper(grid)
+        if b == 0:
+            loads[-1].wait()
         for l in range(depth):
             x = layers_ref[l]
             x = x + change(x, weight)
@@ -304,14 +323,17 @@
     size = half // plane_n
     piece = size // line_n if size % (8 * line_n) == 0 else size
     vmem = pl.BlockSpec(memory_space=pltpu.VMEM)
+    hbm = pl.BlockSpec(memory_space=pltpu.HBM)
     f32 = jnp.float32
     dma = pltpu.SemaphoreType.DMA
     state, prior = pl.pallas_call(
         functools.partial(gather_kernel, tiles, layers),
         out_shape=(jax.ShapeDtypeStruct((depth, members, width), f32), jax.ShapeDtypeStruct((rows, LANES), f32)),
-        in_specs=[pl.BlockSpec(memory_space=pltpu.HBM)] * 6,
-        out_specs=(vmem, vmem),
+        in_specs=[hbm] * 6,
+        out_specs=(hbm, vmem),
         scratch_shapes=[
+            pltpu.VMEM((depth, members, width), f32),
+            dma,
             pltpu.VMEM((members, depth, width), f32),
             *[pltpu.VMEM((depth, width), f32)] * 4,
             pltpu.VMEM((batches, count), jnp.int32),
@@ -332,19 +354,23 @@
             dma((batches, 2 * line_n - 2)),
             dma((batches, 2 * line_n - 2)),
         ],
-        compiler_params=pltpu.CompilerParams(collective_id=0, has_side_effects=True, vmem_limit_bytes=40 * 2**20),
+        compiler_params=pltpu.CompilerParams(collective_id=0, has_side_effects=True, vmem_limit_bytes=63 * 2**20),
         name="gather_prior",
     )(ensemble, diff_x, diff_z, cour_x, cour_z, obs_cell)
     return pl.pallas_call(
         functools.partial(update_kernel, tiles * width, width),
         out_shape=jax.ShapeDtypeStruct((members, depth, width), f32),
-        in_specs=[vmem] * 6,
+        in_specs=[hbm] * 6,
         out_specs=vmem,
         scratch_shapes=[
             pltpu.VMEM((depth, members, width), f32),
             pltpu.VMEM((batches, members, count), f32),
+            pltpu.VMEM((rows, LANES), f32),
+            *[pltpu.VMEM((batches, count), jnp.int32)] * 2,
+            *[pltpu.VMEM((batches, count), f32)] * 2,
+            dma((6,)),
         ],
-        compiler_params=pltpu.CompilerParams(vmem_limit_bytes=40 * 2**20),
+        compiler_params=pltpu.CompilerParams(vmem_limit_bytes=63 * 2**20),
         name="update",
     )(state, prior, obs_cell, obs_radius, obs_value, obs_var)
 

time: 45.6 us -> 42.8 us (0.939)
  local copies, waits for them, and re-layouts: 4.53 us -> 0 us
  Pallas kernels: 40.6 us -> 42.5 us
    unnamed x18 -> x0, local copies, waits for them, and re-layouts: 4.53 us -> none
    pallas_call x1, Pallas kernels: 11.7 us -> 13 us  [shards(): pl.pallas_call(functools.partial(update_kernel, tiles * width, width), ou...]
    pallas_call x1, Pallas kernels: 28.9 us -> 29.6 us  [shards(): pl.pallas_call(functools.partial(gather_kernel, tiles, layers), out_shape...]
where the time goes in v3:
time: 42.8 us; the launch traced here: 42.5 us
  Pallas kernels  42.5 us (99%)
    pallas_call x1, Pallas kernels, shards(): pl.pallas_call(functools.partial(gather_kernel, tiles, layers), out_shape...  29.6 us
    pallas_call x1, Pallas kernels, shards(): pl.pallas_call(functools.partial(update_kernel, tiles * width, width), ou...  13 us

profile of v3, /device:TPU:0, one launch (start us, length us, event | category | flops | bytes accessed | tf_op | source)
XLA Modules:
  0.0 42.5 jit_solution(9981923671193935625)
XLA Ops:
  0.0 29.6 %gather_prior.1 = (f32[4,64,512]{2,1,0:T(8,128)}, f32[1024,128]{1,0:T(8,128)}) custom-call(f32[64,4,512]{2,1,0:T(4,128)} %ens_in.1, f32[4,512]{1,0:T(4,128)} %dx_in.1, f32[4,512]{1,0:T(4,128)} %dz_in.1, f32[4,512]{1,0:T(4,128)} %cx_in.1, f32[4,512]{1,0:T(4,128)} %cz_in.1, s32[4,512]{1,0:T(4,128)} %cell_in.3), custom_call_target="tpu_custom_call" | custom-call | tf_op jit(solution)/shard_map/gather_prior/pallas_call | solution.py:329
  29.6 13.0 %update.1 = f32[64,4,512]{2,1,0:T(4,128)} custom-call(f32[4,64,512]{2,1,0:T(8,128)} %get-tuple-element.7.state_in, f32[1024,128]{1,0:T(8,128)} %get-tuple-element.8.prior_in, s32[4,512]{1,0:T(4,128)} %cell_in.3, s32[4,512]{1,0:T(4,128)} %radius_in.1, f32[4,512]{1,0:T(4,128)} %value_in.1, f32[4,512]{1,0:T(4,128)} %var_in.1), custom_call_target="tpu_custom_call" | custom-call | tf_op jit(solution)/shard_map/update/pallas_call | solution.py:360
